TPU v7x, 512 devices: a whole 4x4x16 slice. The times are simulated.
512 devices in a mesh: vid: 32 (over y, z_lo, core), aud: 16 (over z_hi, x).
Axes of the slice: x: 4, y: 4, z: 16 (z_hi: 4, z_lo: 4; z = z_hi * 4 + z_lo), core: 2. Of those that a mesh axis runs over, the one named last changes fastest.
Arguments:
- video_match: bfloat16 [8192, 1024], P(('vid', 'aud')), may hold values from -6 to 6
- video_value: bfloat16 [8192, 1024], P(('vid', 'aud')), may hold values from -6 to 6
- audio_match: bfloat16 [8192, 1024], P(('vid', 'aud')), may hold values from -6 to 6
- audio_value: bfloat16 [8192, 1024], P(('vid', 'aud')), may hold values from -6 to 6
- video_proj: bfloat16 [1024, 1024], replicated, may hold values from -0.1875 to 0.1875
- audio_proj: bfloat16 [1024, 1024], replicated, may hold values from -0.1875 to 0.1875
Outputs:
- video_out: bfloat16 [8192, 1024], P(('vid', 'aud'))
- audio_out: bfloat16 [8192, 1024], P(('vid', 'aud'))
All inputs are finite; a program needn't handle non-finite values.
Results may differ from a plain program's by a relative error of at most 0.013.
Values may be sent and summed in bfloat16 or wider, within the bound.
A program may use at most 64 MiB of HBM per device.

v0:
```python
import jax
import jax.numpy as jnp
from jax import lax
from jax.sharding import PartitionSpec as P

HEADS = 8
HEAD_DIM = 128


def head_cols(field, head):
    return field[:, head * HEAD_DIM : (head + 1) * HEAD_DIM]


def tile_scores(block, keys, head):
    return lax.dot_general(
        head_cols(block, head),
        head_cols(keys, head),
        (((1,), (1,)), ((), ())),
        preferred_element_type=jnp.float32,
    ) * HEAD_DIM ** (-0.5)


def finish(numer, total, proj):
    rows = numer.shape[0]
    mixed = (
        (numer.reshape(rows, HEADS, HEAD_DIM) / total[..., None])
        .reshape(rows, HEADS * HEAD_DIM)
        .astype(jnp.bfloat16)
    )
    return jnp.dot(mixed, proj, preferred_element_type=jnp.float32).astype(jnp.bfloat16)


def shards(video_match, video_value, audio_match, audio_value, video_proj, audio_proj):
    vid_match, vid_value = (
        lax.all_gather(video_match, "aud", axis=0, tiled=True),
        lax.all_gather(video_value, "aud", axis=0, tiled=True),
    )
    aud_match, aud_value = (
        lax.all_gather(audio_match, "vid", axis=0, tiled=True),
        lax.all_gather(audio_value, "vid", axis=0, tiled=True),
    )
    vblock = vid_match.shape[0]
    ablock = aud_match.shape[0]
    step_rows = min(512, vblock)
    starts = list(range(0, vblock, step_rows))
    row_list = []
    col_top = [jnp.full((ablock,), -jnp.inf, jnp.float32) for head in range(HEADS)]
    for start in starts:
        found = []
        for head in range(HEADS):
            score = tile_scores(vid_match, aud_match, head)
            found.append(score.max(1))
            col_top[head] = score.max(0)
        row_list.append(jnp.stack(found, 1))
    row_top = lax.pmax(row_list[0], "aud")
    col_peak = lax.pmax(jnp.stack(col_top, 1), "vid")
    row_nums, row_sums = ([], [])
    col_sum = [jnp.zeros((ablock,), jnp.float32) for head in range(HEADS)]
    col_num = [jnp.zeros((ablock, HEAD_DIM), jnp.float32) for head in range(HEADS)]
    for start in starts:
        nums, sums = ([], [])
        for head in range(HEADS):
            score = tile_scores(vid_match, aud_match, head)
            row_exp = jnp.exp(score - row_top[start : start + step_rows, head][:, None])
            sums.append(row_exp.sum(1))
            nums.append(
                jnp.dot(
                    row_exp.astype(jnp.bfloat16),
                    head_cols(aud_value, head),
                    preferred_element_type=jnp.float32,
                )
            )
            col_exp = jnp.exp(score - col_peak[:, head][None, :])
            col_sum[head] = col_exp.sum(0)
            col_num[head] = lax.dot_general(
                col_exp.astype(jnp.bfloat16),
                head_cols(vid_value, head),
                (((0,), (0,)), ((), ())),
                preferred_element_type=jnp.float32,
            )
        row_nums.append(jnp.concatenate(nums, 1))
        row_sums.append(jnp.stack(sums, 1))
    video_num, video_sum = (
        lax.psum_scatter(row_nums[0], "aud", scatter_dimension=0, tiled=True),
        lax.psum_scatter(row_sums[0], "aud", scatter_dimension=0, tiled=True),
    )
    audio_num, audio_sum = (
        lax.psum_scatter(jnp.concatenate(col_num, 1), "vid", scatter_dimension=0, tiled=True),
        lax.psum_scatter(jnp.stack(col_sum, 1), "vid", scatter_dimension=0, tiled=True),
    )
    return (finish(video_num, video_sum, video_proj), finish(audio_num, audio_sum, audio_proj))


def solution(mesh):
    return jax.shard_map(
        shards,
        mesh=mesh,
        in_specs=(
            P(("vid", "aud"), None),
            P(("vid", "aud"), None),
            P(("vid", "aud"), None),
            P(("vid", "aud"), None),
            P(),
            P(),
        ),
        out_specs=(P(("vid", "aud"), None), P(("vid", "aud"), None)),
        check_vma=False,
    )
```

profile of v0, /device:TPU:1, one launch (start us, length us, event | category | flops | bytes accessed | tf_op | source)
XLA Modules:
  0.0 803.6 jit_solution(4612141859026334884)
XLA Ops:
  7.2 0.0 all-gather.3.cloned.1.call-start
  7.2 0.7 all-gather.3.cloned.1.call-update
  7.9 0.0 all-gather.5.cloned.1.call-start
  8.0 0.7 all-gather.5.cloned.1.call-update
  8.7 0.0 reduce-scatter.15.cloned.1.call-start
  8.7 56.1 %all_gather.12 = bf16[256,1024]{1,0:T(8,128)(2,1)S(1)} all-gather(bf16[16,1024]{1,0:T(8,128)(2,1)} %param.6), channel_id=1, replica_groups=mesh['vid'=32,'aud'=16] {'aud'}, dimensions={0}, use_global_device_ids=true | all-gather | bytes 557056 | tf_op jit(solution)/shard_map/all_gather | solution.py:35
  64.8 16.5 %all-gather.3.cloned.1.call-done = bf16[512,1024]{1,0:T(8,128)(2,1)} async-done(((bf16[16,1024]{1,0:T(8,128)(2,1)}), bf16[512,1024]{1,0:T(8,128)(2,1)}) %all-gather.3.cloned.1.call-update) | async-done | bytes 1048592 | tf_op jit(solution)/shard_map/all_gather | solution.py:39
  81.3 1.3 fusion.98
  82.6 1.3 fusion.99
  83.9 2.0 fusion.100
  85.9 1.9 fusion.101
  87.8 1.0 fusion.102
  88.8 1.1 fusion.103
  89.9 1.0 fusion.104
  90.9 1.1 fusion.105
  92.0 47.4 %pmax.14 = f32[256,8]{0,1:T(8,128)S(1)} all-reduce(f32[256,8]{0,1:T(8,128)S(1)} %stack.116), channel_id=1, replica_groups=mesh['vid'=32,'aud'=16] {'aud'}, use_global_device_ids=true, to_apply=%region_8.0 | all-reduce | flops 2048 | bytes 16384 | tf_op jit(solution)/shard_map/pmax | solution.py:55
  139.4 134.5 %pmax.15 = f32[512,8]{0,1:T(8,128)S(1)} all-reduce(f32[512,8]{0,1:T(8,128)S(1)} %stack.134), channel_id=1, replica_groups=mesh['vid'=32,'aud'=16] {'vid'}, use_global_device_ids=true, to_apply=%region_27.0 | all-reduce | flops 4096 | bytes 32768 | tf_op jit(solution)/shard_map/pmax | solution.py:56
  274.0 0.2 fusion.30
  274.2 0.2 fusion.32
  274.5 1.4 fusion.28
  275.8 1.3 fusion.26
  277.1 0.2 fusion.24
  277.4 0.2 fusion.22
  277.6 0.2 fusion.20
  277.8 0.2 fusion.18
  278.1 0.8 copy.12
  278.9 0.0 reduce-scatter.15.cloned.1.call-update
  278.9 0.0 reduce-scatter.19.cloned.1.call-start
  279.0 0.8 copy.16
  279.9 0.0 reduce-scatter.19.cloned.1.call-update
  279.9 0.0 reduce-scatter.13.cloned.1.call-start
  279.9 0.0 all-gather.5.cloned.1.call-done
  280.0 2.2 convolution_dynamic-update-slice_fusion.15
  282.2 2.0 convolution_dynamic-update-slice_fusion.14
  284.2 2.0 convolution_dynamic-update-slice_fusion.13
  286.2 1.9 convolution_dynamic-update-slice_fusion.12
  288.1 1.0 convolution_dynamic-update-slice_fusion.11
  289.0 1.0 convolution_dynamic-update-slice_fusion.10
  290.0 0.9 convolution_dynamic-update-slice_fusion.9
  290.9 1.0 convolution_dynamic-update-slice_fusion.8
  291.9 2.5 copy.10
  294.5 0.0 reduce-scatter.17.cloned.1.call-start
  294.6 43.7 %all_gather.15 = bf16[256,1024]{1,0:T(8,128)(2,1)S(1)} all-gather(bf16[16,1024]{1,0:T(8,128)(2,1)S(1)} %copy-done.16), channel_id=1, replica_groups=mesh['vid'=32,'aud'=16] {'aud'}, dimensions={0}, use_global_device_ids=true | all-gather | bytes 557056 | tf_op jit(solution)/shard_map/all_gather | solution.py:36
  338.2 2.1 convolution_dynamic-update-slice_fusion.7
  340.3 2.0 convolution_dynamic-update-slice_fusion.6
  342.3 0.9 convolution_dynamic-update-slice_fusion.5
  343.3 1.0 convolution_dynamic-update-slice_fusion.4
  344.2 1.0 convolution_dynamic-update-slice_fusion.3
  345.2 1.0 convolution_dynamic-update-slice_fusion.2
  346.1 0.9 convolution_dynamic-update-slice_fusion.1
  347.1 1.0 convolution_dynamic-update-slice_fusion
  348.0 2.9 copy.14
  351.0 35.3 %reduce-scatter.15.cloned.1.call-done = f32[16,8]{1,0:T(8,128)} async-done(((f32[256,8]{1,0:T(8,128)}), f32[16,8]{1,0:T(8,128)}) %reduce-scatter.15.cloned.1.call-update) | async-done | bytes 528
  386.3 0.8 copy.13
  387.0 142.6 %reduce-scatter.19.cloned.1.call-done = f32[16,8]{1,0:T(8,128)} async-done(((f32[512,8]{1,0:T(8,128)}), f32[16,8]{1,0:T(8,128)}) %reduce-scatter.19.cloned.1.call-update) | async-done | bytes 528
  529.7 0.8 copy.17
  530.4 116.9 %reduce-scatter.13.cloned.1.call-done = f32[16,1024]{1,0:T(8,128)} async-done(((f32[256,1024]{1,0:T(8,128)}), f32[16,1024]{1,0:T(8,128)}) %reduce-scatter.13.cloned.1.call-update) | async-done | bytes 65552
  647.4 1.0 copy.11
  648.4 0.1 fusion.1
  648.5 1.0 convolution_convert_fusion.1
  649.5 143.6 %reduce-scatter.17.cloned.1.call-done = f32[16,1024]{1,0:T(8,128)} async-done(((f32[512,1024]{1,0:T(8,128)}), f32[16,1024]{1,0:T(8,128)}) %reduce-scatter.17.cloned.1.call-update) | async-done | bytes 65552
  793.1 1.0 copy.15
  794.1 0.1 fusion
  794.2 2.6 convolution_convert_fusion
  (42 shorter events, 0.3 us)
Async XLA Ops:
  7.2 641.3 %copy-start = (bf16[1024,1024]{1,0:T(8,128)(2,1)S(1)}, bf16[1024,1024]{1,0:T(8,128)(2,1)}, u32[]{:S(2)}) copy-start(bf16[1024,1024]{1,0:T(8,128)(2,1)} %param.10) | copy-start | bytes 6291460
  7.2 74.1 %all-gather.3.cloned.1.call-start = ((), (), s32[]{:S(2)}) async-start(), calls=%async_computation.4 | async-start | bytes 1081344 | tf_op jit(solution)/shard_map/all_gather | solution.py:39
  7.9 272.0 %all-gather.5.cloned.1.call-start = ((), (), s32[]{:S(2)}) async-start(), calls=%async_computation.5 | async-start | bytes 1081344 | tf_op jit(solution)/shard_map/all_gather | solution.py:40
  8.7 377.6 %reduce-scatter.15.cloned.1.call-start = ((), (), s32[]{:S(2)}) async-start(), calls=%async_computation.7 | async-start | bytes 139264
  64.8 16.5 %copy-start.12 = (bf16[256,1024]{1,0:T(8,128)(2,1)}, bf16[256,1024]{1,0:T(8,128)(2,1)S(1)}, u32[]{:S(2)}) copy-start(bf16[256,1024]{1,0:T(8,128)(2,1)S(1)} %all_gather.12) | copy-start | bytes 1572868
  81.3 4.6 copy-start.15
  82.6 5.2 copy-start.13
  273.9 3.2 copy-start.5
  273.9 3.4 copy-start.8
  273.9 3.7 copy-start.10
  274.0 3.9 copy-start.11
  278.9 250.8 %reduce-scatter.19.cloned.1.call-start = ((), (), s32[]{:S(2)}) async-start(), calls=%async_computation.9 | async-start | bytes 270336
  279.9 367.5 %reduce-scatter.13.cloned.1.call-start = ((), (), s32[]{:S(2)}) async-start(), calls=%async_computation.6 | async-start | bytes 1114112
  280.0 6.2 copy-start.6
  280.0 8.1 %copy-start.3 = (f32[256,512]{1,0:T(8,128)S(1)}, f32[256,512]{1,0:T(8,128)}, u32[]{:S(2)}) copy-start(f32[256,512]{1,0:T(8,128)} %get-tuple-element.54) | copy-start | bytes 1572868
  280.0 8.1 %copy-start.14 = (bf16[512,1024]{1,0:T(8,128)(2,1)S(1)}, bf16[512,1024]{1,0:T(8,128)(2,1)}, u32[]{:S(2)}) copy-start(bf16[512,1024]{1,0:T(8,128)(2,1)} %all-gather.5.cloned.1.call-done) | copy-start | bytes 3145732
  280.0 9.0 %copy-start.1 = (f32[256,512]{1,0:T(8,128)S(1)}, f32[256,512]{1,0:T(8,128)}, u32[]{:S(2)}) copy-start(f32[256,512]{1,0:T(8,128)} %get-tuple-element.55) | copy-start | bytes 1572868
  290.9 3.6 copy-start.16
  294.5 498.6 %reduce-scatter.17.cloned.1.call-start = ((), (), s32[]{:S(2)}) async-start(), calls=%async_computation.8 | async-start | bytes 2162688
  294.5 47.8 %copy-start.9 = (f32[256,512]{1,0:T(8,128)S(1)}, f32[256,512]{1,0:T(8,128)}, u32[]{:S(2)}) copy-start(f32[256,512]{1,0:T(8,128)} %get-tuple-element.52) | copy-start | bytes 1572868
  294.5 48.7 %copy-start.7 = (f32[256,512]{1,0:T(8,128)S(1)}, f32[256,512]{1,0:T(8,128)}, u32[]{:S(2)}) copy-start(f32[256,512]{1,0:T(8,128)} %get-tuple-element.53) | copy-start | bytes 1572868
  294.5 49.7 %copy-start.4 = (f32[256,512]{1,0:T(8,128)S(1)}, f32[256,512]{1,0:T(8,128)}, u32[]{:S(2)}) copy-start(f32[256,512]{1,0:T(8,128)} %get-tuple-element.54) | copy-start | bytes 1572868
  338.2 6.9 copy-start.2
Sparse Core Ops, SparseCore 0:
  10.2 71.0 all-gather.2
  83.4 62.7 all-gather.4
  279.0 107.1 reduce-scatter.14
  389.1 140.4 reduce-scatter.18
  533.6 113.7 reduce-scatter.12
  650.3 142.7 reduce-scatter.16
where the time goes:
time: 809 us; the launch traced here: 804 us
  waiting for transfers between devices  456 us (56%)
  blocking collectives  282 us (35%)
  matrix products  36 us (4%)
  between operations  14.3 us (2%)
  local copies, waits for them, and re-layouts  10.9 us (1%)
    unnamed x10, waiting for transfers between devices  440 us
    pmax x1, blocking collectives, shards(): col_peak = lax.pmax(jnp.stack(col_top, 1), 'vid')  135 us
    all_gather x1, blocking collectives, shards(): lax.all_gather(video_match, 'aud', axis=0, tiled=True)  56.1 us
    pmax x1, blocking collectives, shards(): row_top = lax.pmax(row_list[0], 'aud')  47.4 us
    all_gather x1, blocking collectives, shards(): lax.all_gather(video_value, 'aud', axis=0, tiled=True)  43.7 us
    all_gather x1, waiting for transfers between devices, shards(): lax.all_gather(audio_match, 'vid', axis=0, tiled=True)  16.5 us
  transfers between devices with their start and end apart: 6, of which 5 were waited for; matrix products, arithmetic and copies ran while one was open for 6% of the time, Pallas kernels for 0%

commit v1 on v0

v1 whole, which is shorter than its diff:
```python
import math

import jax
import jax.numpy as jnp
from jax import lax
from jax.experimental import pallas as pl
from jax.experimental.pallas import tpu as pltpu
from jax.sharding import PartitionSpec as P

MESH = pl.DeviceIdType.MESH
HEADS = 8
DIM = 128
ROWS = 16
BLOCK = HEADS * ROWS
TOKENS = 8 * BLOCK
WIDTH = HEADS * DIM
STAT = BLOCK + 16
CHUNK = 256
SCALE = DIM ** (-0.5) * math.log2(math.e)
F32, BF16 = jnp.float32, jnp.bfloat16
NT = (((1,), (1,)), ((), ()))


def position():
    v, a = lax.axis_index("vid"), lax.axis_index("aud")
    return a % 4, v // 8, (a // 4) * 4 + (v // 2) % 4, v % 2


def device(place):
    x, y, z, c = place
    return ((y * 4 + z % 4) * 2 + c, (z // 4) * 4 + x)


def head_peer(place, k):
    x, y, z, c = place
    return x, y, (z + 2 * k + 16) % 16, c


def video_peer(place, k):
    x, y, z, c = place
    step = k // 2 if k >= 0 else -((-k) // 2)
    return (x + step + 4) % 4, y, z, (c + k) % 2 if k >= 0 else (c - k) % 2


def audio_peer(place, k):
    x, y, z, c = place
    step = k // 2 if k >= 0 else -((-k) // 2)
    return x, (y + step + 4) % 4, (z // 2) * 2 + (z + abs(k)) % 2, c


def send(src, dst, sems, n, place):
    return pltpu.make_async_remote_copy(
        src_ref=src,
        dst_ref=dst,
        send_sem=sems.at[0, n],
        recv_sem=sems.at[1, n],
        device_id=device(place),
        device_id_type=MESH,
    )


def attend(side, tile, values_t, out):
    keys = tile[:, 2 - 2 * side].reshape(TOKENS, DIM)

    def chunk(i, carry):
        slots = CHUNK // BLOCK
        queries = tile[pl.ds(i * slots, slots), 2 * side].reshape(CHUNK, DIM)
        score = lax.dot_general(keys, queries, NT, preferred_element_type=F32)
        peak = score.max(0, keepdims=True).astype(BF16).astype(F32)
        weight = jnp.exp2((score - peak) * SCALE)
        total = weight.sum(0, keepdims=True)
        num = jnp.dot(values_t[...], weight.astype(BF16), preferred_element_type=F32)
        high = total.astype(BF16).astype(F32)
        row = lax.broadcasted_iota(jnp.int32, (16, CHUNK), 0)
        stat = jnp.where(row == 0, peak, jnp.where(row == 1, high, jnp.where(row == 2, total - high, 0.0)))
        for s in range(slots):
            lanes = slice(s * BLOCK, (s + 1) * BLOCK)
            out[side, i * slots + s, :BLOCK] = num[:, lanes].astype(BF16)
            out[side, i * slots + s, BLOCK:] = stat[:, lanes].astype(BF16)
        return carry

    lax.fori_loop(0, TOKENS // CHUNK, chunk, 0)


def combine(side, part, back, mixed):
    def source(k):
        return part if k == 0 else back

    stats = [source(k)[side, k, BLOCK:].astype(F32) for k in range(8)]
    peaks = [s[0:1] for s in stats]
    top = peaks[0]
    for p in peaks[1:]:
        top = jnp.maximum(top, p)
    num = jnp.zeros((DIM, BLOCK), F32)
    total = jnp.zeros((1, BLOCK), F32)
    for k in range(8):
        gain = jnp.exp2((peaks[k] - top) * SCALE)
        total = total + gain * (stats[k][1:2] + stats[k][2:3])
        num = num + gain * source(k)[side, k, :BLOCK].astype(F32)
    mix = (num / total).T.astype(BF16)
    mixed[:, side] = mix.reshape(HEADS, ROWS, DIM)


def kernel(vm, vv, am, av, vproj, aproj, vout, aout,
           staged, tile, values_t, part, back, mixed, whole, weights,
           head_sems, gather_sems, return_sems, final_sems, local_sems):
    place = position()
    head = place[2] // 2

    loads = [
        pltpu.make_async_copy(vproj, weights.at[0], local_sems.at[0]),
        pltpu.make_async_copy(aproj, weights.at[1], local_sems.at[1]),
    ]
    for load in loads:
        load.start()

    barrier = pltpu.get_barrier_semaphore()
    for peer in (head_peer, video_peer, audio_peer):
        for k in range(1, 8):
            pl.semaphore_signal(barrier, inc=1, device_id=device(peer(place, k)), device_id_type=MESH)
    for n, array in enumerate((vm, vv, am, av)):
        for h in range(HEADS):
            staged[h, n] = array[:, h * DIM : (h + 1) * DIM]
    tile[0, :, :ROWS] = staged[head]
    pl.semaphore_wait(barrier, 21)

    sends = []
    for k in range(1, 8):
        peer = head_peer(place, k)
        sends.append(send(staged.at[peer[2] // 2], tile.at[0, :, pl.ds(k * ROWS, ROWS)], head_sems, k, peer))
    for s in sends:
        s.start()
    for s in sends:
        s.wait_recv()

    gathers = []
    for k in range(1, 8):
        gathers.append(send(tile.at[0, pl.ds(0, 2)], tile.at[k, pl.ds(0, 2)], gather_sems, k, video_peer(place, k)))
        gathers.append(send(tile.at[0, pl.ds(2, 2)], tile.at[k, pl.ds(2, 2)], gather_sems, 8 + k, audio_peer(place, k)))
    for s in gathers:
        s.start()
    for s in gathers:
        s.wait_recv()

    returns = []
    for side, peer in ((0, video_peer), (1, audio_peer)):
        for k in range(8):
            values_t[:, k * BLOCK : (k + 1) * BLOCK] = tile[k, 3 - 2 * side].T
        attend(side, tile, values_t, part)
        for k in range(1, 8):
            returns.append(send(part.at[side, k], back.at[side, k], return_sems, 8 * side + k, peer(place, -k)))
            returns[-1].start()
    for side in range(2):
        for s in returns[7 * side : 7 * side + 7]:
            s.wait_recv()
        combine(side, part, back, mixed)

    finals = []
    for k in range(1, 8):
        finals.append(send(mixed.at[k], whole.at[head], final_sems, k, head_peer(place, -k)))
        finals[-1].start()
    whole[head] = mixed[0]
    for load in loads:
        load.wait()
    for k, s in enumerate(finals):
        s.wait_recv()
    for side, out in ((0, vout), (1, aout)):
        mix = jnp.concatenate([whole[h, side] for h in range(HEADS)], axis=1)
        out[...] = jnp.dot(mix, weights[side], preferred_element_type=F32).astype(BF16)
    for s in sends + gathers + returns + finals:
        s.wait_send()


def shards(*args):
    vmem = pl.BlockSpec(memory_space=pltpu.VMEM)
    hbm = pl.BlockSpec(memory_space=pl.ANY)
    return pl.pallas_call(
        kernel,
        out_shape=[jax.ShapeDtypeStruct((ROWS, WIDTH), BF16)] * 2,
        in_specs=[vmem] * 4 + [hbm] * 2,
        out_specs=[vmem] * 2,
        scratch_shapes=[
            pltpu.VMEM((HEADS, 4, ROWS, DIM), BF16),
            pltpu.VMEM((8, 4, BLOCK, DIM), BF16),
            pltpu.VMEM((DIM, TOKENS), BF16),
            pltpu.VMEM((2, 8, STAT, DIM), BF16),
            pltpu.VMEM((2, 8, STAT, DIM), BF16),
            pltpu.VMEM((HEADS, 2, ROWS, DIM), BF16),
            pltpu.VMEM((HEADS, 2, ROWS, DIM), BF16),
            pltpu.VMEM((2, WIDTH, WIDTH), BF16),
            pltpu.SemaphoreType.DMA((2, 8)),
            pltpu.SemaphoreType.DMA((2, 16)),
            pltpu.SemaphoreType.DMA((2, 16)),
            pltpu.SemaphoreType.DMA((2, 8)),
            pltpu.SemaphoreType.DMA((2,)),
        ],
        compiler_params=pltpu.CompilerParams(
            collective_id=0, has_side_effects=True, vmem_limit_bytes=40 * 2**20
        ),
    )(*args)


def solution(mesh):
    tokens = P(("vid", "aud"), None)
    return jax.shard_map(
        shards,
        mesh=mesh,
        in_specs=(tokens,) * 4 + (P(), P()),
        out_specs=(tokens, tokens),
        check_vma=False,
    )
```

time: 809 us -> 64.6 us (0.08)
  waiting for transfers between devices: 456 us -> 0 us
  blocking collectives: 282 us -> 0 us
  Pallas kernels: 0 us -> 55.3 us
  matrix products: 36 us -> 0 us
  between operations: 14.3 us -> 0.65 us
    unnamed x10 -> x0, waiting for transfers between devices: 440 us -> none
    pmax x2 -> x0, blocking collectives: 182 us -> none  [the longest x1 135 us: shards(): col_peak = lax.pmax(jnp.stack(col_top, 1), 'vid')]
    all_gather x2 -> x0, blocking collectives: 99.8 us -> none  [the longest x1 56.1 us: shards(): lax.all_gather(video_match, 'aud', axis=0, tiled=True)]
    pallas_call x0 -> x1, Pallas kernels: none -> 55.3 us  [shards(): pl.pallas_call(kernel, out_shape=[jax.ShapeDtypeStruct((ROWS, WIDTH), BF1...]
    dot_general x26 -> x0, matrix products: 36 us -> none  [the longest x8 11.9 us: shards(): jnp.dot(row_exp.astype(jnp.bfloat16), head_cols(aud_value, head), preferr...]
    all_gather x2 -> x0, waiting for transfers between devices: 16.5 us -> none  [the longest x1 16.5 us: shards(): lax.all_gather(audio_match, 'vid', axis=0, tiled=True)]
  transfers between devices with their start and end apart: 6 -> 0, of which waited for: 5 -> 0; matrix products, arithmetic and copies ran while one was open for 6% -> 0% of each run, Pallas kernels for 0% -> 0%
where the time goes in v1:
time: 64.6 us; the launch traced here: 63.4 us
  Pallas kernels  55.3 us (86%)
  local copies, waits for them, and re-layouts  7.44 us (12%)
  between operations  0.65 us (1%)
    pallas_call x1, Pallas kernels, shards(): pl.pallas_call(kernel, out_shape=[jax.ShapeDtypeStruct((ROWS, WIDTH), BF1...  55.3 us
    unnamed x14, local copies, waits for them, and re-layouts  7.44 us

profile of v1, /device:TPU:1, one launch (start us, length us, event | category | flops | bytes accessed | tf_op | source)
XLA Modules:
  0.0 63.4 jit_solution(969583978307958325)
XLA Ops:
  0.6 0.0 copy-start
  0.6 1.6 %copy-done = bf16[1024,1024]{1,0:T(8,128)(2,1)S(1)} copy-done((bf16[1024,1024]{1,0:T(8,128)(2,1)S(1)}, bf16[1024,1024]{1,0:T(8,128)(2,1)}, u32[]{:S(2)}) %copy-start) | copy-done | bytes 2097176
  2.2 0.0 copy-start.1
  2.2 1.6 %copy-done.1 = bf16[1024,1024]{1,0:T(8,128)(2,1)S(1)} copy-done((bf16[1024,1024]{1,0:T(8,128)(2,1)S(1)}, bf16[1024,1024]{1,0:T(8,128)(2,1)}, u32[]{:S(2)}) %copy-start.1) | copy-done | bytes 2097176
  3.8 0.0 copy-start.2
  3.8 0.8 %copy-done.2 = bf16[16,1024]{1,0:T(8,128)(2,1)S(1)} copy-done((bf16[16,1024]{1,0:T(8,128)(2,1)S(1)}, bf16[16,1024]{1,0:T(8,128)(2,1)}, u32[]{:S(2)}) %copy-start.2) | copy-done | bytes 32792
  4.6 0.0 copy-start.3
  4.6 0.8 %copy-done.3 = bf16[16,1024]{1,0:T(8,128)(2,1)S(1)} copy-done((bf16[16,1024]{1,0:T(8,128)(2,1)S(1)}, bf16[16,1024]{1,0:T(8,128)(2,1)}, u32[]{:S(2)}) %copy-start.3) | copy-done | bytes 32792
  5.3 0.0 copy-start.4
  5.3 0.8 %copy-done.4 = bf16[16,1024]{1,0:T(8,128)(2,1)S(1)} copy-done((bf16[16,1024]{1,0:T(8,128)(2,1)S(1)}, bf16[16,1024]{1,0:T(8,128)(2,1)}, u32[]{:S(2)}) %copy-start.4) | copy-done | bytes 32792
  6.1 0.0 copy-start.5
  6.1 0.8 %copy-done.5 = bf16[16,1024]{1,0:T(8,128)(2,1)S(1)} copy-done((bf16[16,1024]{1,0:T(8,128)(2,1)S(1)}, bf16[16,1024]{1,0:T(8,128)(2,1)}, u32[]{:S(2)}) %copy-start.5) | copy-done | bytes 32792
  6.8 55.3 %shard_map.77 = (bf16[16,1024]{1,0:T(8,128)(2,1)S(1)}, bf16[16,1024]{1,0:T(8,128)(2,1)S(1)}) custom-call(bf16[16,1024]{1,0:T(8,128)(2,1)S(1)} %copy-done.2, bf16[16,1024]{1,0:T(8,128)(2,1)S(1)} %copy-done.3, bf16[16,1024]{1,0:T(8,128)(2,1)S(1)} %copy-done.4, bf16[16,1024]{1,0:T(8,128)(2,1)S(1)} %copy-done.5, bf16[1024,1024]{1,0:T(8,128)(2,1)S(1)} %copy-done, ...), custom_call_target="tpu_custom_call" | custom-call | tf_op jit(solution)/shard_map/pallas_call | solution.py:177
  62.2 0.6 copy.10
  62.8 0.6 copy.11
Async XLA Ops:
  0.6 1.6 %copy-start = (bf16[1024,1024]{1,0:T(8,128)(2,1)S(1)}, bf16[1024,1024]{1,0:T(8,128)(2,1)}, u32[]{:S(2)}) copy-start(bf16[1024,1024]{1,0:T(8,128)(2,1)} %vproj.1) | copy-start | bytes 6291460
  2.2 1.6 %copy-start.1 = (bf16[1024,1024]{1,0:T(8,128)(2,1)S(1)}, bf16[1024,1024]{1,0:T(8,128)(2,1)}, u32[]{:S(2)}) copy-start(bf16[1024,1024]{1,0:T(8,128)(2,1)} %aproj.1) | copy-start | bytes 6291460
  3.8 0.8 %copy-start.2 = (bf16[16,1024]{1,0:T(8,128)(2,1)S(1)}, bf16[16,1024]{1,0:T(8,128)(2,1)}, u32[]{:S(2)}) copy-start(bf16[16,1024]{1,0:T(8,128)(2,1)} %vm.1) | copy-start | bytes 98308
  4.6 0.8 %copy-start.3 = (bf16[16,1024]{1,0:T(8,128)(2,1)S(1)}, bf16[16,1024]{1,0:T(8,128)(2,1)}, u32[]{:S(2)}) copy-start(bf16[16,1024]{1,0:T(8,128)(2,1)} %vv.1) | copy-start | bytes 98308
  5.3 0.8 %copy-start.4 = (bf16[16,1024]{1,0:T(8,128)(2,1)S(1)}, bf16[16,1024]{1,0:T(8,128)(2,1)}, u32[]{:S(2)}) copy-start(bf16[16,1024]{1,0:T(8,128)(2,1)} %am.1) | copy-start | bytes 98308
  6.1 0.8 %copy-start.5 = (bf16[16,1024]{1,0:T(8,128)(2,1)S(1)}, bf16[16,1024]{1,0:T(8,128)(2,1)}, u32[]{:S(2)}) copy-start(bf16[16,1024]{1,0:T(8,128)(2,1)} %av.1) | copy-start | bytes 98308

commit v2 on v1

v2 whole, which is shorter than its diff:
```python
import math

import jax
import jax.numpy as jnp
from jax import lax
from jax.experimental import pallas as pl
from jax.experimental.pallas import tpu as pltpu
from jax.sharding import PartitionSpec as P

MESH = pl.DeviceIdType.MESH
HEADS = 8
DIM = 128
ROWS = 16
BLOCK = HEADS * ROWS
TOKENS = 8 * BLOCK
WIDTH = HEADS * DIM
STAT = BLOCK + 16
PAIR = 2
CHUNK = PAIR * BLOCK
ORDER = (0, 1, 7, 2, 6, 3, 5, 4)
PARTS = ((0, 5), (5, 8))
SCALE = DIM ** (-0.5) * math.log2(math.e)
F32, BF16 = jnp.float32, jnp.bfloat16
NT = (((1,), (1,)), ((), ()))


def position():
    v, a = lax.axis_index("vid"), lax.axis_index("aud")
    return a % 4, v // 8, (a // 4) * 4 + (v // 2) % 4, v % 2


def device(place):
    x, y, z, c = place
    return ((y * 4 + z % 4) * 2 + c, (z // 4) * 4 + x)


def head_peer(place, k):
    x, y, z, c = place
    return x, y, (z + 2 * k + 16) % 16, c


def video_peer(place, k):
    x, y, z, c = place
    step = k // 2 if k >= 0 else -((-k) // 2)
    return (x + step + 4) % 4, y, z, (c + k) % 2 if k >= 0 else (c - k) % 2


def audio_peer(place, k):
    x, y, z, c = place
    step = k // 2 if k >= 0 else -((-k) // 2)
    return x, (y + step + 4) % 4, (z // 2) * 2 + (z + abs(k)) % 2, c


def send(src, dst, sems, n, place):
    return pltpu.make_async_remote_copy(
        src_ref=src,
        dst_ref=dst,
        send_sem=sems.at[0, n],
        recv_sem=sems.at[1, n],
        device_id=device(place),
        device_id_type=MESH,
    )


def attend(side, slot, tile, values_t, out):
    keys = tile[:, 2 - 2 * side].reshape(TOKENS, DIM)
    queries = tile[slot : slot + PAIR, 2 * side].reshape(CHUNK, DIM)
    score = lax.dot_general(keys, queries, NT, preferred_element_type=F32)
    peak = score.max(0, keepdims=True).astype(BF16).astype(F32)
    weight = jnp.exp2((score - peak) * SCALE)
    total = weight.sum(0, keepdims=True)
    num = jnp.dot(values_t[...], weight.astype(BF16), preferred_element_type=F32)
    high = total.astype(BF16).astype(F32)
    row = lax.broadcasted_iota(jnp.int32, (16, CHUNK), 0)
    stat = jnp.where(row == 0, peak, jnp.where(row == 1, high, jnp.where(row == 2, total - high, 0.0)))
    for s in range(PAIR):
        lanes = slice(s * BLOCK, (s + 1) * BLOCK)
        out[side, slot + s, :BLOCK] = num[:, lanes].astype(BF16)
        out[side, slot + s, BLOCK:] = stat[:, lanes].astype(BF16)


def combine(side, part, back, mixed):
    def source(k):
        return part if k == 0 else back

    stats = [source(k)[side, k, BLOCK:].astype(F32) for k in range(8)]
    peaks = [s[0:1] for s in stats]
    top = peaks[0]
    for p in peaks[1:]:
        top = jnp.maximum(top, p)
    num = jnp.zeros((DIM, BLOCK), F32)
    total = jnp.zeros((1, BLOCK), F32)
    for k in range(8):
        gain = jnp.exp2((peaks[k] - top) * SCALE)
        total = total + gain * (stats[k][1:2] + stats[k][2:3])
        num = num + gain * source(k)[side, k, :BLOCK].astype(F32)
    mix = (num / total).T.astype(BF16)
    mixed[side] = mix.reshape(HEADS, ROWS, DIM)


def kernel(vm, vv, am, av, vproj, aproj, vout, aout,
           tokens, staged, tile, values_t, part, back, mixed, whole, weights,
           head_sems, gather_sems, return_sems, final_sems, local_sems):
    place = position()
    head = place[2] // 2

    loads = [
        pltpu.make_async_copy(array, tokens.at[n], local_sems.at[n]) for n, array in enumerate((vm, vv, am, av))
    ] + [
        pltpu.make_async_copy(array, weights.at[n], local_sems.at[4 + n]) for n, array in enumerate((vproj, aproj))
    ]
    for load in loads:
        load.start()

    barrier = pltpu.get_barrier_semaphore()
    for peer in (head_peer, video_peer, audio_peer):
        for k in range(1, 8):
            pl.semaphore_signal(barrier, inc=1, device_id=device(peer(place, k)), device_id_type=MESH)
    for n in range(4):
        loads[n].wait()
        for h in range(HEADS):
            staged[h, n] = tokens[n, :, h * DIM : (h + 1) * DIM]
    tile[0, :, :ROWS] = staged[head]
    pl.semaphore_wait(barrier, 21)

    sends = {}
    for k in (4, 3, 5, 2, 6, 1, 7):
        peer = head_peer(place, k)
        rows = pl.ds(ORDER.index(k) * ROWS, ROWS)
        sends[k] = send(staged.at[peer[2] // 2], tile.at[0, :, rows], head_sems, k, peer)
        sends[k].start()

    gathers = []
    for n, (first, last) in enumerate(PARTS):
        for k in ORDER[first:last]:
            if k:
                sends[k].wait_recv()
        rows = pl.ds(first * ROWS, (last - first) * ROWS)
        for k in (4, 5, 2, 3, 6, 7, 1):
            for side, peer in ((0, video_peer), (1, audio_peer)):
                arrays = pl.ds(2 * side, 2)
                gathers.append(
                    send(tile.at[0, arrays, rows], tile.at[k, arrays, rows], gather_sems, 16 * n + 8 * side + k, peer(place, k))
                )
                gathers[-1].start()
    for s in gathers:
        s.wait_recv()

    returns = [[], []]
    for side, peer in ((0, video_peer), (1, audio_peer)):
        for k in range(8):
            values_t[:, k * BLOCK : (k + 1) * BLOCK] = tile[k, 3 - 2 * side].T
        for slot in range(8 - PAIR, -1, -PAIR):
            attend(side, slot, tile, values_t, part)
            for k in range(slot, slot + PAIR):
                if k:
                    returns[side].append(
                        send(part.at[side, k], back.at[side, k], return_sems, 8 * side + k, peer(place, -k))
                    )
                    returns[side][-1].start()

    finals = [[], []]
    for side in range(2):
        for s in returns[side]:
            s.wait_recv()
        combine(side, part, back, mixed)
        for k in (4, 3, 5, 2, 6, 1, 7):
            peer = head_peer(place, -k)
            finals[side].append(
                send(mixed.at[side, ORDER.index(k)], whole.at[side, head], final_sems, 8 * side + k, peer)
            )
            finals[side][-1].start()
        whole[side, head] = mixed[side, 0]
    for load in loads[4:]:
        load.wait()
    for side, out in ((0, vout), (1, aout)):
        for s in finals[side]:
            s.wait_recv()
        mix = jnp.concatenate([whole[side, h] for h in range(HEADS)], axis=1)
        out[...] = jnp.dot(mix, weights[side], preferred_element_type=F32).astype(BF16)
    for s in [*sends.values(), *gathers, *returns[0], *returns[1], *finals[0], *finals[1]]:
        s.wait_send()


def shards(*args):
    vmem = pl.BlockSpec(memory_space=pltpu.VMEM)
    hbm = pl.BlockSpec(memory_space=pl.ANY)
    return pl.pallas_call(
        kernel,
        out_shape=[jax.ShapeDtypeStruct((ROWS, WIDTH), BF16)] * 2,
        in_specs=[hbm] * 6,
        out_specs=[vmem] * 2,
        scratch_shapes=[
            pltpu.VMEM((4, ROWS, WIDTH), BF16),
            pltpu.VMEM((HEADS, 4, ROWS, DIM), BF16),
            pltpu.VMEM((8, 4, BLOCK, DIM), BF16),
            pltpu.VMEM((DIM, TOKENS), BF16),
            pltpu.VMEM((2, 8, STAT, DIM), BF16),
            pltpu.VMEM((2, 8, STAT, DIM), BF16),
            pltpu.VMEM((2, HEADS, ROWS, DIM), BF16),
            pltpu.VMEM((2, HEADS, ROWS, DIM), BF16),
            pltpu.VMEM((2, WIDTH, WIDTH), BF16),
            pltpu.SemaphoreType.DMA((2, 8)),
            pltpu.SemaphoreType.DMA((2, 16 * len(PARTS))),
            pltpu.SemaphoreType.DMA((2, 16)),
            pltpu.SemaphoreType.DMA((2, 16)),
            pltpu.SemaphoreType.DMA((6,)),
        ],
        compiler_params=pltpu.CompilerParams(
            collective_id=0, has_side_effects=True, vmem_limit_bytes=60 * 2**20
        ),
    )(*args)


def solution(mesh):
    tokens = P(("vid", "aud"), None)
    return jax.shard_map(
        shards,
        mesh=mesh,
        in_specs=(tokens,) * 4 + (P(), P()),
        out_specs=(tokens, tokens),
        check_vma=False,
    )
```

time: 64.6 us -> 54.6 us (0.85); the launches traced: 63.4 us -> 54.3 us
  local copies, waits for them, and re-layouts: 7.44 us -> 2.75 us
  Pallas kernels: 55.3 us -> 50.9 us
    unnamed x14 -> x2, local copies, waits for them, and re-layouts: 7.44 us -> 2.75 us
    pallas_call x1, Pallas kernels: 55.3 us -> 50.9 us  [shards(): pl.pallas_call(kernel, out_shape=[jax.ShapeDtypeStruct((ROWS, WIDTH), BF1...]
where the time goes in v2:
time: 54.6 us; the launch traced here: 54.3 us
  Pallas kernels  50.9 us (93%)
  local copies, waits for them, and re-layouts  2.75 us (5%)
  between operations  0.64 us (1%)
    pallas_call x1, Pallas kernels, shards(): pl.pallas_call(kernel, out_shape=[jax.ShapeDtypeStruct((ROWS, WIDTH), BF1...  50.9 us
    unnamed x2, local copies, waits for them, and re-layouts  2.75 us

profile of v2, /device:TPU:1, one launch (start us, length us, event | category | flops | bytes accessed | tf_op | source)
XLA Modules:
  0.0 54.3 jit_solution(10792265656991390456)
XLA Ops:
  0.6 50.9 %shard_map.77 = (bf16[16,1024]{1,0:T(8,128)(2,1)}, bf16[16,1024]{1,0:T(8,128)(2,1)}) custom-call(bf16[16,1024]{1,0:T(8,128)(2,1)} %vm.1, bf16[16,1024]{1,0:T(8,128)(2,1)} %vv.1, bf16[16,1024]{1,0:T(8,128)(2,1)} %am.1, bf16[16,1024]{1,0:T(8,128)(2,1)} %av.1, bf16[1024,1024]{1,0:T(8,128)(2,1)} %vproj.1, bf16[1024,1024]{1,0:T(8,128)(2,1)} %aproj.1), custom_call_target="tpu_custom_call" | custom-call | tf_op jit(solution)/shard_map/pallas_call | solution.py:188
  51.6 1.4 %copy.10 = bf16[16,1024]{1,0:T(8,128)(2,1)} copy(bf16[16,1024]{1,0:T(8,128)(2,1)} %get-tuple-element.4) | data formatting | bytes 65536
  52.9 1.4 %copy.11 = bf16[16,1024]{1,0:T(8,128)(2,1)} copy(bf16[16,1024]{1,0:T(8,128)(2,1)} %get-tuple-element.5) | data formatting | bytes 65536

commit v3 on v2

v3 whole, which is shorter than its diff:
```python
import math

import jax
import jax.numpy as jnp
from jax import lax
from jax.experimental import pallas as pl
from jax.experimental.pallas import tpu as pltpu
from jax.sharding import PartitionSpec as P

MESH = pl.DeviceIdType.MESH
HEADS = 8
DIM = 128
ROWS = 16
BLOCK = HEADS * ROWS
TOKENS = 8 * BLOCK
WIDTH = HEADS * DIM
STAT = BLOCK + 16
KERNEL_VMEM = 32 * 2**20
FIRST = (4, 1, 7, 2, 6, 3, 5)
WIDE = 4
STEP = 2
ORDER = (0, 1, 7, 2, 6, 3, 5, 4)
PARTS = ((0, 0, 5), (0, 5, 8), (1, 0, 5), (1, 5, 8))
SCALE = DIM ** (-0.5) * math.log2(math.e)
F32, BF16 = jnp.float32, jnp.bfloat16
NT = (((1,), (1,)), ((), ()))


def position():
    v, a = lax.axis_index("vid"), lax.axis_index("aud")
    return a % 4, v // 8, (a // 4) * 4 + (v // 2) % 4, v % 2


def device(place):
    x, y, z, c = place
    return ((y * 4 + z % 4) * 2 + c, (z // 4) * 4 + x)


def head_peer(place, k):
    x, y, z, c = place
    return x, y, (z + 2 * k + 16) % 16, c


def video_peer(place, k):
    x, y, z, c = place
    step = k // 2 if k >= 0 else -((-k) // 2)
    return (x + step + 4) % 4, y, z, (c + k) % 2 if k >= 0 else (c - k) % 2


def audio_peer(place, k):
    x, y, z, c = place
    step = k // 2 if k >= 0 else -((-k) // 2)
    return x, (y + step + 4) % 4, (z // 2) * 2 + (z + abs(k)) % 2, c


def send(src, dst, sems, n, place):
    return pltpu.make_async_remote_copy(
        src_ref=src,
        dst_ref=dst,
        send_sem=sems.at[0, n],
        recv_sem=sems.at[1, n],
        device_id=device(place),
        device_id_type=MESH,
    )


def weigh(side, first, tile, probs):
    lanes = pl.ds(first * BLOCK, WIDE * BLOCK)
    queries = tile[first : first + WIDE, 0, side].reshape(WIDE * BLOCK, DIM)

    def score(n):
        keys = tile[n : n + STEP, 0, 1 - side].reshape(STEP * BLOCK, DIM)
        return lax.dot_general(keys, queries, NT, preferred_element_type=F32)

    peak = None
    for n in range(0, 8, STEP):
        top = score(n).reshape(STEP * BLOCK // 8, 8, WIDE * BLOCK).max(0)
        peak = top if peak is None else jnp.maximum(peak, top)
    peak = peak.max(0, keepdims=True).astype(BF16).astype(F32)
    for n in range(0, 8, STEP):
        weight = jnp.exp2((score(n) - peak) * SCALE)
        probs[side, n * BLOCK : (n + STEP) * BLOCK, lanes] = weight.astype(BF16)
    return peak


def gather_values(side, first, peak, values_t, probs, out):
    num = jnp.dot(values_t[side], probs[side, :, first * BLOCK : (first + WIDE) * BLOCK], preferred_element_type=F32)
    total = num[DIM : DIM + 1]
    high = total.astype(BF16).astype(F32)
    row = lax.broadcasted_iota(jnp.int32, (16, WIDE * BLOCK), 0)
    stat = jnp.where(row == 0, peak, jnp.where(row == 1, high, jnp.where(row == 2, total - high, 0.0)))
    for s in range(WIDE):
        lanes = slice(s * BLOCK, (s + 1) * BLOCK)
        out[side, first + s, :BLOCK] = num[:DIM, lanes].astype(BF16)
        out[side, first + s, BLOCK:] = stat[:, lanes].astype(BF16)


def combine(side, part, back, mixed):
    def source(k):
        return part if k == 0 else back

    stats = [source(k)[side, k, BLOCK:].astype(F32) for k in range(8)]
    peaks = [s[0:1] for s in stats]
    top = peaks[0]
    for p in peaks[1:]:
        top = jnp.maximum(top, p)
    num = jnp.zeros((DIM, BLOCK), F32)
    total = jnp.zeros((1, BLOCK), F32)
    for k in range(8):
        gain = jnp.exp2((peaks[k] - top) * SCALE)
        total = total + gain * (stats[k][1:2] + stats[k][2:3])
        num = num + gain * source(k)[side, k, :BLOCK].astype(F32)
    mix = (num / total).T.astype(BF16)
    mixed[side] = mix.reshape(HEADS, ROWS, DIM)


def kernel(vm, vv, am, av, vproj, aproj, whole, vweights, aweights,
           tokens, staged, tile, values_t, probs, part, back, mixed, mixes,
           head_sems, gather_sems, return_sems, final_sems, local_sems):
    place = position()
    head = place[2] // 2
    loads = [
        pltpu.make_async_copy(array, tokens.at[n], local_sems.at[n]) for n, array in enumerate((vm, am, vv, av))
    ] + [
        pltpu.make_async_copy(vproj, vweights, local_sems.at[4]),
        pltpu.make_async_copy(aproj, aweights, local_sems.at[5]),
    ]
    for load in loads:
        load.start()

    barrier = pltpu.get_barrier_semaphore()
    for peer in (head_peer, video_peer, audio_peer):
        for k in range(1, 8):
            pl.semaphore_signal(barrier, inc=1, device_id=device(peer(place, k)), device_id_type=MESH)
    for n in range(4):
        loads[n].wait()
        for h in range(HEADS):
            staged[n // 2, h, n % 2] = tokens[n, :, h * DIM : (h + 1) * DIM]
    for kind in range(2):
        tile[0, kind, :, :ROWS] = staged[kind, head]
    values_t[:, DIM:] = jnp.ones((2, 16, TOKENS), BF16)
    pl.semaphore_wait(barrier, 21)

    sends = {}
    for kind in range(2):
        for k in FIRST:
            peer = head_peer(place, k)
            rows = pl.ds(ORDER.index(k) * ROWS, ROWS)
            sends[kind, k] = send(staged.at[kind, peer[2] // 2], tile.at[0, kind, :, rows], head_sems, 8 * kind + k, peer)
            sends[kind, k].start()

    gathers = {}
    for n, (kind, first, last) in enumerate(PARTS):
        for k in ORDER[first:last]:
            if k:
                sends[kind, k].wait_recv()
        rows = pl.ds(first * ROWS, (last - first) * ROWS)
        for k in (1, 4, 5, 2, 3, 6, 7):
            for side, peer in ((1, audio_peer), (0, video_peer)):
                sem = 16 * n + 8 * side + k
                gathers[n, side, k] = send(
                    tile.at[0, kind, side, rows], tile.at[k, kind, side, rows], gather_sems, sem, peer(place, k)
                )
                gathers[n, side, k].start()

    def arrive(kind):
        for n, side, k in gathers:
            if PARTS[n][0] == kind:
                gathers[n, side, k].wait_recv()

    arrive(0)
    peaks = {}
    for first in range(8 - WIDE, -1, -WIDE):
        for side in range(2):
            peaks[side, first] = weigh(side, first, tile, probs)
    arrive(1)
    for side in range(2):
        for k in range(8):
            values_t[side, :DIM, k * BLOCK : (k + 1) * BLOCK] = tile[k, 1, 1 - side].T
    returns = {}
    for first in range(8 - WIDE, -1, -WIDE):
        for side, peer in ((0, video_peer), (1, audio_peer)):
            gather_values(side, first, peaks[side, first], values_t, probs, part)
            for k in range(first, first + WIDE):
                if k:
                    returns[side, k] = send(part.at[side, k], back.at[side, k], return_sems, 8 * side + k, peer(place, -k))
                    returns[side, k].start()

    finals = {}
    for side in range(2):
        for k in range(1, 8):
            returns[side, k].wait_recv()
        combine(side, part, back, mixed)
        for k in (4, 3, 5, 2, 6, 1, 7):
            finals[side, k] = send(
                mixed.at[side, ORDER.index(k)], mixes.at[side, head], final_sems, 8 * side + k, head_peer(place, -k)
            )
            finals[side, k].start()
        mixes[side, head] = mixed[side, 0]
    for side in range(2):
        for k in range(1, 8):
            finals[side, k].wait_recv()
        for h in range(HEADS):
            whole[side, :, h * DIM : (h + 1) * DIM] = mixes[side, h]
    for load in loads[4:]:
        load.wait()
    for group in (sends, gathers, returns, finals):
        for s in group.values():
            s.wait_send()


def project(mix, vproj, aproj, vout, aout):
    for side, weights, out in ((0, vproj, vout), (1, aproj, aout)):
        out[...] = jnp.dot(mix[side], weights[...], preferred_element_type=F32).astype(BF16)


def shards(vm, vv, am, av, vproj, aproj):
    vmem = pl.BlockSpec(memory_space=pltpu.VMEM)
    hbm = pl.BlockSpec(memory_space=pltpu.HBM)
    held = pl.pallas_call(
        kernel,
        out_shape=[pltpu.VMEM((2, ROWS, WIDTH), BF16)] + [pltpu.VMEM((WIDTH, WIDTH), BF16)] * 2,
        in_specs=[hbm] * 6,
        out_specs=[vmem] * 3,
        scratch_shapes=[
            pltpu.VMEM((4, ROWS, WIDTH), BF16),
            pltpu.VMEM((2, HEADS, 2, ROWS, DIM), BF16),
            pltpu.VMEM((8, 2, 2, BLOCK, DIM), BF16),
            pltpu.VMEM((2, DIM + 16, TOKENS), BF16),
            pltpu.VMEM((2, TOKENS, TOKENS), BF16),
            pltpu.VMEM((2, 8, STAT, DIM), BF16),
            pltpu.VMEM((2, 8, STAT, DIM), BF16),
            pltpu.VMEM((2, HEADS, ROWS, DIM), BF16),
            pltpu.VMEM((2, HEADS, ROWS, DIM), BF16),
            pltpu.SemaphoreType.DMA((2, 16)),
            pltpu.SemaphoreType.DMA((2, 16 * len(PARTS))),
            pltpu.SemaphoreType.DMA((2, 16)),
            pltpu.SemaphoreType.DMA((2, 16)),
            pltpu.SemaphoreType.DMA((6,)),
        ],
        compiler_params=pltpu.CompilerParams(
            collective_id=0, has_side_effects=True, vmem_limit_bytes=KERNEL_VMEM
        ),
        name="attend",
    )(*(pltpu.with_memory_space_constraint(x, pltpu.HBM) for x in (vm, vv, am, av, vproj, aproj)))
    return pl.pallas_call(
        project,
        out_shape=[jax.ShapeDtypeStruct((ROWS, WIDTH), BF16)] * 2,
        in_specs=[vmem] * 3,
        out_specs=[vmem] * 2,
        compiler_params=pltpu.CompilerParams(vmem_limit_bytes=16 * 2**20),
        name="project",
    )(*(pltpu.with_memory_space_constraint(x, pltpu.VMEM) for x in held))


def solution(mesh):
    tokens = P(("vid", "aud"), None)
    return jax.shard_map(
        shards,
        mesh=mesh,
        in_specs=(tokens,) * 4 + (P(), P()),
        out_specs=(tokens, tokens),
        check_vma=False,
    )
```

time: 54.6 us -> 50.1 us (0.918)
  local copies, waits for them, and re-layouts: 2.75 us -> 0 us
  Pallas kernels: 50.9 us -> 49.4 us
    unnamed x2 -> x0, local copies, waits for them, and re-layouts: 2.75 us -> none
    pallas_call x1 -> x2, Pallas kernels: 50.9 us -> 49.4 us  [the longest x1 48.1 us: shards(): pl.pallas_call(kernel, out_shape=[pltpu.VMEM((2, ROWS, WIDTH), BF16)] + [...]
where the time goes in v3:
time: 50.1 us; the launch traced here: 50 us
  Pallas kernels  49.4 us (99%)
  between operations  0.64 us (1%)
    pallas_call x1, Pallas kernels, shards(): pl.pallas_call(kernel, out_shape=[pltpu.VMEM((2, ROWS, WIDTH), BF16)] + [...  48.1 us
    pallas_call x1, Pallas kernels, shards(): pl.pallas_call(project, out_shape=[jax.ShapeDtypeStruct((ROWS, WIDTH), BF...  1.28 us

profile of v3, /device:TPU:1, one launch (start us, length us, event | category | flops | bytes accessed | tf_op | source)
XLA Modules:
  0.0 50.0 jit_solution(11886236239628398718)
XLA Ops:
  0.6 48.1 %attend.1 = (bf16[2,16,1024]{2,1,0:T(8,128)(2,1)S(1)}, bf16[1024,1024]{1,0:T(8,128)(2,1)S(1)}, bf16[1024,1024]{1,0:T(8,128)(2,1)S(1)}) custom-call(bf16[16,1024]{1,0:T(8,128)(2,1)} %vm.1, bf16[16,1024]{1,0:T(8,128)(2,1)} %vv.1, bf16[16,1024]{1,0:T(8,128)(2,1)} %am.1, bf16[16,1024]{1,0:T(8,128)(2,1)} %av.1, bf16[1024,1024]{1,0:T(8,128)(2,1)} %vproj.1, ...), custom_call_target="tpu_custom_call" | custom-call | tf_op jit(solution)/shard_map/attend/pallas_call | solution.py:220
  48.7 1.3 %project.1 = (bf16[16,1024]{1,0:T(8,128)(2,1)}, bf16[16,1024]{1,0:T(8,128)(2,1)}) custom-call(bf16[2,16,1024]{2,1,0:T(8,128)(2,1)S(1)} %get-tuple-element.5.mix, bf16[1024,1024]{1,0:T(8,128)(2,1)S(1)} %get-tuple-element.6.vproj, bf16[1024,1024]{1,0:T(8,128)(2,1)S(1)} %get-tuple-element.7.aproj), custom_call_target="tpu_custom_call" | custom-call | tf_op jit(solution)/shard_map/project/pallas_call | solution.py:246

commit v4 on v3

--- a/solution.py
+++ b/solution.py
@@ -64,27 +64,48 @@
     )
 
 
-def weigh(side, first, tile, probs):
-    lanes = pl.ds(first * BLOCK, WIDE * BLOCK)
-    queries = tile[first : first + WIDE, 0, side].reshape(WIDE * BLOCK, DIM)
-
-    def score(n):
-        keys = tile[n : n + STEP, 0, 1 - side].reshape(STEP * BLOCK, DIM)
+def weigh(tile, tops, probs):
+    wide, step = WIDE * BLOCK, STEP * BLOCK
+
+    def score(n, first):
+        keys = tile[n : n + STEP, 0, 1].reshape(step, DIM)
+        queries = tile[first : first + WIDE, 0, 0].reshape(wide, DIM)
         return lax.dot_general(keys, queries, NT, preferred_element_type=F32)
 
-    peak = None
+    peaks = [{}, {}]
+    for first in range(0, 8, WIDE):
+        peak = None
+        for n in range(0, 8, STEP):
+            tops_of = pl.ds(n * BLOCK, step)
+            scores = score(n, first)
+            top = scores.reshape(step // 8, 8, wide).max(0)
+            peak = top if peak is None else jnp.maximum(peak, top)
+            top = scores[:, :BLOCK]
+            for s in range(1, WIDE):
+                top = jnp.maximum(top, scores[:, s * BLOCK : (s + 1) * BLOCK])
+            tops[tops_of] = jnp.maximum(tops[tops_of], top) if first else top
+        peaks[0][first] = peak.max(0, keepdims=True).astype(BF16).astype(F32)
     for n in range(0, 8, STEP):
-        top = score(n).reshape(STEP * BLOCK // 8, 8, WIDE * BLOCK).max(0)
-        peak = top if peak is None else jnp.maximum(peak, top)
-    peak = peak.max(0, keepdims=True).astype(BF16).astype(F32)
-    for n in range(0, 8, STEP):
-        weight = jnp.exp2((score(n) - peak) * SCALE)
-        probs[side, n * BLOCK : (n + STEP) * BLOCK, lanes] = weight.astype(BF16)
-    return peak
+        rows = slice(n * BLOCK, n * BLOCK + step)
+        across = tops[rows].max(1, keepdims=True).astype(BF16).astype(F32)
+        for first in range(0, 8, WIDE):
+            lanes = slice(first * BLOCK, first * BLOCK + wide)
+            scores = score(n, first)
+            probs[0, rows, lanes] = jnp.exp2((scores - peaks[0][first]) * SCALE).astype(BF16)
+            probs[1, rows, lanes] = jnp.exp2((scores - across) * SCALE).astype(BF16)
+    for first in range(0, 8, WIDE):
+        peaks[1][first] = jnp.concatenate(
+            [tops[n * BLOCK : (n + 1) * BLOCK].T.max(0, keepdims=True) for n in range(first, first + WIDE)], axis=1
+        ).astype(BF16).astype(F32)
+    return peaks
 
 
 def gather_values(side, first, peak, values_t, probs, out):
-    num = jnp.dot(values_t[side], probs[side, :, first * BLOCK : (first + WIDE) * BLOCK], preferred_element_type=F32)
+    tokens = slice(first * BLOCK, (first + WIDE) * BLOCK)
+    if side:
+        num = lax.dot_general(values_t[1], probs[1, tokens], NT, preferred_element_type=F32)
+    else:
+        num = jnp.dot(values_t[0], probs[0, :, tokens], preferred_element_type=F32)
     total = num[DIM : DIM + 1]
     high = total.astype(BF16).astype(F32)
     row = lax.broadcasted_iota(jnp.int32, (16, WIDE * BLOCK), 0)
@@ -115,7 +136,7 @@
 
 
 def kernel(vm, vv, am, av, vproj, aproj, whole, vweights, aweights,
-           tokens, staged, tile, values_t, probs, part, back, mixed, mixes,
+           tokens, staged, tile, values_t, tops, probs, part, back, mixed, mixes,
            head_sems, gather_sems, return_sems, final_sems, local_sems):
     place = position()
     head = place[2] // 2
@@ -169,10 +190,7 @@
                 gathers[n, side, k].wait_recv()
 
     arrive(0)
-    peaks = {}
-    for first in range(8 - WIDE, -1, -WIDE):
-        for side in range(2):
-            peaks[side, first] = weigh(side, first, tile, probs)
+    peaks = weigh(tile, tops, probs)
     arrive(1)
     for side in range(2):
         for k in range(8):
@@ -180,14 +198,14 @@
     returns = {}
     for first in range(8 - WIDE, -1, -WIDE):
         for side, peer in ((0, video_peer), (1, audio_peer)):
-            gather_values(side, first, peaks[side, first], values_t, probs, part)
+            gather_values(side, first, peaks[side][first], values_t, probs, part)
             for k in range(first, first + WIDE):
                 if k:
                     returns[side, k] = send(part.at[side, k], back.at[side, k], return_sems, 8 * side + k, peer(place, -k))
                     returns[side, k].start()
 
     finals = {}
-    for side in range(2):
+    for side in (1, 0):
         for k in range(1, 8):
             returns[side, k].wait_recv()
         combine(side, part, back, mixed)
@@ -227,6 +245,7 @@
             pltpu.VMEM((2, HEADS, 2, ROWS, DIM), BF16),
             pltpu.VMEM((8, 2, 2, BLOCK, DIM), BF16),
             pltpu.VMEM((2, DIM + 16, TOKENS), BF16),
+            pltpu.VMEM((TOKENS, BLOCK), F32),
             pltpu.VMEM((2, TOKENS, TOKENS), BF16),
             pltpu.VMEM((2, 8, STAT, DIM), BF16),
             pltpu.VMEM((2, 8, STAT, DIM), BF16),

time: 50.1 us -> 49.3 us (0.984)
  Pallas kernels: 49.4 us -> 48.5 us
    pallas_call x1, Pallas kernels: 48.1 us -> 47.3 us  [shards(): pl.pallas_call(kernel, out_shape=[pltpu.VMEM((2, ROWS, WIDTH), BF16)] + [...]
where the time goes in v4:
time: 49.3 us; the launch traced here: 49.2 us
  Pallas kernels  48.5 us (98%)
  between operations  0.64 us (1%)
    pallas_call x1, Pallas kernels, shards(): pl.pallas_call(kernel, out_shape=[pltpu.VMEM((2, ROWS, WIDTH), BF16)] + [...  47.3 us
    pallas_call x1, Pallas kernels, shards(): pl.pallas_call(project, out_shape=[jax.ShapeDtypeStruct((ROWS, WIDTH), BF...  1.28 us

profile of v4, /device:TPU:1, one launch (start us, length us, event | category | flops | bytes accessed | tf_op | source)
XLA Modules:
  0.0 49.2 jit_solution(14864505347345452724)
XLA Ops:
  0.6 47.3 %attend.1 = (bf16[2,16,1024]{2,1,0:T(8,128)(2,1)S(1)}, bf16[1024,1024]{1,0:T(8,128)(2,1)S(1)}, bf16[1024,1024]{1,0:T(8,128)(2,1)S(1)}) custom-call(bf16[16,1024]{1,0:T(8,128)(2,1)} %vm.1, bf16[16,1024]{1,0:T(8,128)(2,1)} %vv.1, bf16[16,1024]{1,0:T(8,128)(2,1)} %am.1, bf16[16,1024]{1,0:T(8,128)(2,1)} %av.1, bf16[1024,1024]{1,0:T(8,128)(2,1)} %vproj.1, ...), custom_call_target="tpu_custom_call" | custom-call | tf_op jit(solution)/shard_map/attend/pallas_call | solution.py:238
  47.9 1.3 %project.1 = (bf16[16,1024]{1,0:T(8,128)(2,1)}, bf16[16,1024]{1,0:T(8,128)(2,1)}) custom-call(bf16[2,16,1024]{2,1,0:T(8,128)(2,1)S(1)} %get-tuple-element.5.mix, bf16[1024,1024]{1,0:T(8,128)(2,1)S(1)} %get-tuple-element.6.vproj, bf16[1024,1024]{1,0:T(8,128)(2,1)S(1)} %get-tuple-element.7.aproj), custom_call_target="tpu_custom_call" | custom-call | tf_op jit(solution)/shard_map/project/pallas_call | solution.py:265

commit v5 on v4

--- a/solution.py
+++ b/solution.py
@@ -16,11 +16,10 @@
 WIDTH = HEADS * DIM
 STAT = BLOCK + 16
 KERNEL_VMEM = 32 * 2**20
-FIRST = (4, 1, 7, 2, 6, 3, 5)
 WIDE = 4
 STEP = 2
 ORDER = (0, 1, 7, 2, 6, 3, 5, 4)
-PARTS = ((0, 0, 5), (0, 5, 8), (1, 0, 5), (1, 5, 8))
+PARTS = ((None, 0, 5), (0, 5, 8), (1, 5, 8))
 SCALE = DIM ** (-0.5) * math.log2(math.e)
 F32, BF16 = jnp.float32, jnp.bfloat16
 NT = (((1,), (1,)), ((), ()))
@@ -136,8 +135,8 @@
 
 
 def kernel(vm, vv, am, av, vproj, aproj, whole, vweights, aweights,
-           tokens, staged, tile, values_t, tops, probs, part, back, mixed, mixes,
-           head_sems, gather_sems, return_sems, final_sems, local_sems):
+           tokens, staged, passing, tile, values_t, tops, probs, part, back, mixed, mixes,
+           pass_sems, head_sems, gather_sems, return_sems, final_sems, local_sems):
     place = position()
     head = place[2] // 2
     loads = [
@@ -150,9 +149,9 @@
         load.start()
 
     barrier = pltpu.get_barrier_semaphore()
-    for peer in (head_peer, video_peer, audio_peer):
-        for k in range(1, 8):
-            pl.semaphore_signal(barrier, inc=1, device_id=device(peer(place, k)), device_id_type=MESH)
+    greeted = [(head_peer, k) for k in (2, 6, 1, 7)] + [(peer, k) for peer in (video_peer, audio_peer) for k in range(1, 8)]
+    for peer, k in greeted:
+        pl.semaphore_signal(barrier, inc=1, device_id=device(peer(place, k)), device_id_type=MESH)
     for n in range(4):
         loads[n].wait()
         for h in range(HEADS):
@@ -160,33 +159,66 @@
     for kind in range(2):
         tile[0, kind, :, :ROWS] = staged[kind, head]
     values_t[:, DIM:] = jnp.ones((2, 16, TOKENS), BF16)
-    pl.semaphore_wait(barrier, 21)
-
-    sends = {}
+    pl.semaphore_wait(barrier, len(greeted))
+
+    def rows_of(k):
+        return pl.ds(ORDER.index(k) * ROWS, ROWS)
+
+    def columns(kind, k):
+        return staged.at[kind, (head + k) % HEADS]
+
+    legs, sends = {}, {}
+    for kind in (0,):
+        for n, (src, dst, via) in enumerate((
+            (columns(kind, 4).at[0], passing.at[kind, 2, 0], 2),
+            (columns(kind, 4).at[1], passing.at[kind, 2, 1], -2),
+            (columns(kind, 3), passing.at[kind, 0], 2),
+            (columns(kind, 5), passing.at[kind, 1], -2),
+        )):
+            legs[kind, n] = send(src, dst, pass_sems, 4 * kind + n, head_peer(place, via))
+            legs[kind, n].start()
+    for k in (1, 7, 2, 6):
+        sends[k] = send(
+            staged.at[:, (head + k) % HEADS], tile.at[0, :, :, rows_of(k)], head_sems, k, head_peer(place, k)
+        )
+        sends[k].start()
+    for kind in (1,):
+        for n, (src, dst, via) in enumerate((
+            (columns(kind, 4).at[0], passing.at[kind, 2, 0], 2),
+            (columns(kind, 4).at[1], passing.at[kind, 2, 1], -2),
+            (columns(kind, 3), passing.at[kind, 0], 2),
+            (columns(kind, 5), passing.at[kind, 1], -2),
+        )):
+            legs[kind, n] = send(src, dst, pass_sems, 4 * kind + n, head_peer(place, via))
+            legs[kind, n].start()
     for kind in range(2):
-        for k in FIRST:
-            peer = head_peer(place, k)
-            rows = pl.ds(ORDER.index(k) * ROWS, ROWS)
-            sends[kind, k] = send(staged.at[kind, peer[2] // 2], tile.at[0, kind, :, rows], head_sems, 8 * kind + k, peer)
-            sends[kind, k].start()
+        for n, (src, dst, to) in enumerate((
+            (passing.at[kind, 2, 0], tile.at[0, kind, 0, rows_of(4)], 2),
+            (passing.at[kind, 2, 1], tile.at[0, kind, 1, rows_of(4)], -2),
+            (passing.at[kind, 0], tile.at[0, kind, :, rows_of(3)], 1),
+            (passing.at[kind, 1], tile.at[0, kind, :, rows_of(5)], -1),
+        )):
+            legs[kind, n].wait_recv()
+            sends[kind, n] = send(src, dst, head_sems, 8 + 4 * kind + n, head_peer(place, to))
+            sends[kind, n].start()
 
     gathers = {}
     for n, (kind, first, last) in enumerate(PARTS):
-        for k in ORDER[first:last]:
-            if k:
-                sends[kind, k].wait_recv()
+        for key in (2, 6, 1, 7) if kind is None else ((kind, 0), (kind, 1), (kind, 2), (kind, 3)):
+            sends[key].wait_recv()
         rows = pl.ds(first * ROWS, (last - first) * ROWS)
+        kinds = slice(None) if kind is None else kind
         for k in (1, 4, 5, 2, 3, 6, 7):
             for side, peer in ((1, audio_peer), (0, video_peer)):
                 sem = 16 * n + 8 * side + k
                 gathers[n, side, k] = send(
-                    tile.at[0, kind, side, rows], tile.at[k, kind, side, rows], gather_sems, sem, peer(place, k)
+                    tile.at[0, kinds, side, rows], tile.at[k, kinds, side, rows], gather_sems, sem, peer(place, k)
                 )
                 gathers[n, side, k].start()
 
     def arrive(kind):
         for n, side, k in gathers:
-            if PARTS[n][0] == kind:
+            if (PARTS[n][0] or 0) == kind:
                 gathers[n, side, k].wait_recv()
 
     arrive(0)
@@ -222,7 +254,7 @@
             whole[side, :, h * DIM : (h + 1) * DIM] = mixes[side, h]
     for load in loads[4:]:
         load.wait()
-    for group in (sends, gathers, returns, finals):
+    for group in (legs, sends, gathers, returns, finals):
         for s in group.values():
             s.wait_send()
 
@@ -243,6 +275,7 @@
         scratch_shapes=[
             pltpu.VMEM((4, ROWS, WIDTH), BF16),
             pltpu.VMEM((2, HEADS, 2, ROWS, DIM), BF16),
+            pltpu.VMEM((2, 3, 2, ROWS, DIM), BF16),
             pltpu.VMEM((8, 2, 2, BLOCK, DIM), BF16),
             pltpu.VMEM((2, DIM + 16, TOKENS), BF16),
             pltpu.VMEM((TOKENS, BLOCK), F32),
@@ -251,6 +284,7 @@
             pltpu.VMEM((2, 8, STAT, DIM), BF16),
             pltpu.VMEM((2, HEADS, ROWS, DIM), BF16),
             pltpu.VMEM((2, HEADS, ROWS, DIM), BF16),
+            pltpu.SemaphoreType.DMA((2, 8)),
             pltpu.SemaphoreType.DMA((2, 16)),
             pltpu.SemaphoreType.DMA((2, 16 * len(PARTS))),
             pltpu.SemaphoreType.DMA((2, 16)),

time: 49.3 us -> 47.8 us (0.970)
  Pallas kernels: 48.5 us -> 47.1 us
    pallas_call x1, Pallas kernels: 47.3 us -> 45.8 us  [shards(): pl.pallas_call(kernel, out_shape=[pltpu.VMEM((2, ROWS, WIDTH), BF16)] + [...]
where the time goes in v5:
time: 47.8 us; the launch traced here: 47.7 us
  Pallas kernels  47.1 us (99%)
  between operations  0.64 us (1%)
    pallas_call x1, Pallas kernels, shards(): pl.pallas_call(kernel, out_shape=[pltpu.VMEM((2, ROWS, WIDTH), BF16)] + [...  45.8 us
    pallas_call x1, Pallas kernels, shards(): pl.pallas_call(project, out_shape=[jax.ShapeDtypeStruct((ROWS, WIDTH), BF...  1.28 us

profile of v5, /device:TPU:1, one launch (start us, length us, event | category | flops | bytes accessed | tf_op | source)
XLA Modules:
  0.0 47.7 jit_solution(10370917104008265878)
XLA Ops:
  0.6 45.8 %attend.1 = (bf16[2,16,1024]{2,1,0:T(8,128)(2,1)S(1)}, bf16[1024,1024]{1,0:T(8,128)(2,1)S(1)}, bf16[1024,1024]{1,0:T(8,128)(2,1)S(1)}) custom-call(bf16[16,1024]{1,0:T(8,128)(2,1)} %vm.1, bf16[16,1024]{1,0:T(8,128)(2,1)} %vv.1, bf16[16,1024]{1,0:T(8,128)(2,1)} %am.1, bf16[16,1024]{1,0:T(8,128)(2,1)} %av.1, bf16[1024,1024]{1,0:T(8,128)(2,1)} %vproj.1, ...), custom_call_target="tpu_custom_call" | custom-call | tf_op jit(solution)/shard_map/attend/pallas_call | solution.py:270
  46.4 1.3 %project.1 = (bf16[16,1024]{1,0:T(8,128)(2,1)}, bf16[16,1024]{1,0:T(8,128)(2,1)}) custom-call(bf16[2,16,1024]{2,1,0:T(8,128)(2,1)S(1)} %get-tuple-element.5.mix, bf16[1024,1024]{1,0:T(8,128)(2,1)S(1)} %get-tuple-element.6.vproj, bf16[1024,1024]{1,0:T(8,128)(2,1)S(1)} %get-tuple-element.7.aproj), custom_call_target="tpu_custom_call" | custom-call | tf_op jit(solution)/shard_map/project/pallas_call | solution.py:299

commit v6 on v5

--- a/solution.py
+++ b/solution.py
@@ -139,6 +139,10 @@
            pass_sems, head_sems, gather_sems, return_sems, final_sems, local_sems):
     place = position()
     head = place[2] // 2
+    barrier = pltpu.get_barrier_semaphore()
+    greeted = [(head_peer, k) for k in (2, 6, 1, 7)] + [(peer, k) for peer in (video_peer, audio_peer) for k in range(1, 8)]
+    for peer, k in greeted:
+        pl.semaphore_signal(barrier, inc=1, device_id=device(peer(place, k)), device_id_type=MESH)
     loads = [
         pltpu.make_async_copy(array, tokens.at[n], local_sems.at[n]) for n, array in enumerate((vm, am, vv, av))
     ] + [
@@ -148,10 +152,6 @@
     for load in loads:
         load.start()
 
-    barrier = pltpu.get_barrier_semaphore()
-    greeted = [(head_peer, k) for k in (2, 6, 1, 7)] + [(peer, k) for peer in (video_peer, audio_peer) for k in range(1, 8)]
-    for peer, k in greeted:
-        pl.semaphore_signal(barrier, inc=1, device_id=device(peer(place, k)), device_id_type=MESH)
     for n in range(4):
         loads[n].wait()
         for h in range(HEADS):
@@ -208,7 +208,7 @@
             sends[key].wait_recv()
         rows = pl.ds(first * ROWS, (last - first) * ROWS)
         kinds = slice(None) if kind is None else kind
-        for k in (1, 4, 5, 2, 3, 6, 7):
+        for k in (5, 4, 3, 7, 2, 6, 1):
             for side, peer in ((1, audio_peer), (0, video_peer)):
                 sem = 16 * n + 8 * side + k
                 gathers[n, side, k] = send(
@@ -231,7 +231,7 @@
     for first in range(8 - WIDE, -1, -WIDE):
         for side, peer in ((0, video_peer), (1, audio_peer)):
             gather_values(side, first, peaks[side][first], values_t, probs, part)
-            for k in range(first, first + WIDE):
+            for k in (first + 1, first, first + 3, first + 2):
                 if k:
                     returns[side, k] = send(part.at[side, k], back.at[side, k], return_sems, 8 * side + k, peer(place, -k))
                     returns[side, k].start()

time: 47.8 us -> 47.5 us (level)
  no operation moved by 1% of the time
where the time goes in v6:
time: 47.5 us; the launch traced here: 47.4 us
  Pallas kernels  46.8 us (99%)
  between operations  0.64 us (1%)
    pallas_call x1, Pallas kernels, shards(): pl.pallas_call(kernel, out_shape=[pltpu.VMEM((2, ROWS, WIDTH), BF16)] + [...  45.5 us
    pallas_call x1, Pallas kernels, shards(): pl.pallas_call(project, out_shape=[jax.ShapeDtypeStruct((ROWS, WIDTH), BF...  1.28 us

profile of v6, /device:TPU:1, one launch (start us, length us, event | category | flops | bytes accessed | tf_op | source)
XLA Modules:
  0.0 47.4 jit_solution(3877853153659707813)
XLA Ops:
  0.6 45.5 %attend.1 = (bf16[2,16,1024]{2,1,0:T(8,128)(2,1)S(1)}, bf16[1024,1024]{1,0:T(8,128)(2,1)S(1)}, bf16[1024,1024]{1,0:T(8,128)(2,1)S(1)}) custom-call(bf16[16,1024]{1,0:T(8,128)(2,1)} %vm.1, bf16[16,1024]{1,0:T(8,128)(2,1)} %vv.1, bf16[16,1024]{1,0:T(8,128)(2,1)} %am.1, bf16[16,1024]{1,0:T(8,128)(2,1)} %av.1, bf16[1024,1024]{1,0:T(8,128)(2,1)} %vproj.1, ...), custom_call_target="tpu_custom_call" | custom-call | tf_op jit(solution)/shard_map/attend/pallas_call | solution.py:270
  46.1 1.3 %project.1 = (bf16[16,1024]{1,0:T(8,128)(2,1)}, bf16[16,1024]{1,0:T(8,128)(2,1)}) custom-call(bf16[2,16,1024]{2,1,0:T(8,128)(2,1)S(1)} %get-tuple-element.5.mix, bf16[1024,1024]{1,0:T(8,128)(2,1)S(1)} %get-tuple-element.6.vproj, bf16[1024,1024]{1,0:T(8,128)(2,1)S(1)} %get-tuple-element.7.aproj), custom_call_target="tpu_custom_call" | custom-call | tf_op jit(solution)/shard_map/project/pallas_call | solution.py:299

commit v7 on v6

--- a/solution.py
+++ b/solution.py
@@ -259,9 +259,14 @@
             s.wait_send()
 
 
-def project(mix, vproj, aproj, vout, aout):
+def project(mix, vproj, aproj, vout, aout, held, sems):
+    copies = []
     for side, weights, out in ((0, vproj, vout), (1, aproj, aout)):
-        out[...] = jnp.dot(mix[side], weights[...], preferred_element_type=F32).astype(BF16)
+        held[side] = jnp.dot(mix[side], weights[...], preferred_element_type=F32).astype(BF16)
+        copies.append(pltpu.make_async_copy(held.at[side], out, sems.at[side]))
+        copies[-1].start()
+    for copy in copies:
+        copy.wait()
 
 
 def shards(vm, vv, am, av, vproj, aproj):
@@ -300,7 +305,8 @@
         project,
         out_shape=[jax.ShapeDtypeStruct((ROWS, WIDTH), BF16)] * 2,
         in_specs=[vmem] * 3,
-        out_specs=[vmem] * 2,
+        out_specs=[pl.BlockSpec(memory_space=pl.ANY)] * 2,
+        scratch_shapes=[pltpu.VMEM((2, ROWS, WIDTH), BF16), pltpu.SemaphoreType.DMA((2,))],
         compiler_params=pltpu.CompilerParams(vmem_limit_bytes=16 * 2**20),
         name="project",
     )(*(pltpu.with_memory_space_constraint(x, pltpu.VMEM) for x in held))

time: 47.5 us -> 47.5 us (level)
  no operation moved by 1% of the time
where the time goes in v7:
time: 47.5 us; the launch traced here: 47.4 us
  Pallas kernels  46.8 us (99%)
  between operations  0.64 us (1%)
    pallas_call x1, Pallas kernels, shards(): pl.pallas_call(kernel, out_shape=[pltpu.VMEM((2, ROWS, WIDTH), BF16)] + [...  45.5 us
    pallas_call x1, Pallas kernels, shards(): pl.pallas_call(project, out_shape=[jax.ShapeDtypeStruct((ROWS, WIDTH), BF...  1.3 us

profile of v7, /device:TPU:1, one launch (start us, length us, event | category | flops | bytes accessed | tf_op | source)
XLA Modules:
  0.0 47.4 jit_solution(13652999366996775213)
XLA Ops:
  0.6 45.5 %attend.1 = (bf16[2,16,1024]{2,1,0:T(8,128)(2,1)S(1)}, bf16[1024,1024]{1,0:T(8,128)(2,1)S(1)}, bf16[1024,1024]{1,0:T(8,128)(2,1)S(1)}) custom-call(bf16[16,1024]{1,0:T(8,128)(2,1)} %vm.1, bf16[16,1024]{1,0:T(8,128)(2,1)} %vv.1, bf16[16,1024]{1,0:T(8,128)(2,1)} %am.1, bf16[16,1024]{1,0:T(8,128)(2,1)} %av.1, bf16[1024,1024]{1,0:T(8,128)(2,1)} %vproj.1, ...), custom_call_target="tpu_custom_call" | custom-call | tf_op jit(solution)/shard_map/attend/pallas_call | solution.py:275
  46.1 1.3 %project.1 = (bf16[16,1024]{1,0:T(8,128)(2,1)}, bf16[16,1024]{1,0:T(8,128)(2,1)}) custom-call(bf16[2,16,1024]{2,1,0:T(8,128)(2,1)S(1)} %get-tuple-element.5.mix, bf16[1024,1024]{1,0:T(8,128)(2,1)S(1)} %get-tuple-element.6.vproj, bf16[1024,1024]{1,0:T(8,128)(2,1)S(1)} %get-tuple-element.7.aproj), custom_call_target="tpu_custom_call" | custom-call | tf_op jit(solution)/shard_map/project/pallas_call | solution.py:304
